TPU v7x, 256 devices: a whole 4x4x8 slice. The times are simulated.
256 devices in a mesh: row: 32 (over y, z_hi, core), col: 8 (over z_lo, x).
Axes of the slice: x: 4, y: 4, z: 8 (z_hi: 4, z_lo: 2; z = z_hi * 2 + z_lo), core: 2. Of those that a mesh axis runs over, the one named last changes fastest.
Arguments:
- pair_elems: bfloat16 [12288, 20000], P(('row', 'col')), may hold values from -0.5 to 0.5
- pair_bands: int32 [2, 12288], P(None, ('row', 'col')), may hold values from 0 to 255, as said below
- valence_energy: float32 [48], replicated, may hold values from -4 to -0.5
- conduction_energy: float32 [256], replicated, may hold values from 0.5 to 5
Outputs:
- polar_slab: float32 [2048, 20000], P('col', 'row')
Inputs may be any that keep to these rules, and one draw needn't show every extreme that they name: `pair_bands`: each of the 12288 valence-conduction pairs appears exactly once; row 0 holds valence indices below 48, row 1 conduction indices below 256.
All inputs are finite; a program needn't handle non-finite values.
Results may differ from a plain program's by a relative error of at most 0.0024.
Values may be sent and summed in bfloat16 or wider, within the bound.
A program may use at most 128 MiB of HBM per device.

v0:
```python
import jax
import jax.numpy as jnp
from jax import lax
from jax.sharding import PartitionSpec as P

NCOL = 2048


def pair_weights(band_table, valence_energy, conduction_energy):
    valence_ids = jnp.arange(valence_energy.shape[0], dtype=jnp.int32)
    conduct_ids = jnp.arange(conduction_energy.shape[0], dtype=jnp.int32)
    valence_level = jnp.sum(
        jnp.where(
            band_table[0][:, None] == valence_ids[None, :],
            valence_energy[None, :],
            jnp.float32(0.0),
        ),
        axis=1,
    )
    conduct_level = jnp.sum(
        jnp.where(
            band_table[1][:, None] == conduct_ids[None, :],
            conduction_energy[None, :],
            jnp.float32(0.0),
        ),
        axis=1,
    )
    return -4.0 / (conduct_level - valence_level)


def shards(pair_elems, pair_bands, valence_energy, conduction_energy):
    weights = pair_weights(pair_bands, valence_energy, conduction_energy)
    weighted = (weights[:, None] * pair_elems[:, :NCOL].astype(jnp.float32)).astype(jnp.bfloat16)
    row_block = lax.all_to_all(pair_elems, "row", split_axis=1, concat_axis=0, tiled=True)
    contract_first = (((0,), (0,)), ((), ()))
    slab_group = lax.all_gather(weighted, "row", axis=0, tiled=True)
    panels = lax.all_to_all(slab_group, "col", split_axis=1, concat_axis=0, tiled=True)
    return lax.dot_general(
        panels,
        lax.all_gather(row_block, "col", axis=0, tiled=True),
        contract_first,
        preferred_element_type=jnp.float32,
    )


def solution(mesh):
    placed = (P(("row", "col"), None), P(None, ("row", "col")), P(), P())
    return jax.shard_map(
        shards, mesh=mesh, in_specs=placed, out_specs=P("col", "row"), check_vma=False
    )
```

profile of v0, /device:TPU:1, one launch (start us, length us, event | category | flops | bytes accessed | tf_op | source)
XLA Modules:
  0.0 360.7 jit_solution(6065620434501281692)
XLA Ops:
  6.5 0.0 all-gather.3.cloned.1.call-start
  6.5 0.8 slice_bitcast_fusion
  7.3 0.8 select_reduce_fusion.1
  8.1 0.9 select_reduce_fusion
  9.0 1.7 multiply_convert_fusion
  10.7 0.0 all-gather.3.cloned.1.call-update
  10.7 0.0 all-gather.5.cloned.1.call-start
  10.8 5.7 %all_to_all.32 = bf16[48,32,625]{2,1,0:T(8,128)(2,1)S(1)} reshape(bf16[48,20000]{1,0:T(8,128)(2,1)} %param.4) | data formatting | bytes 3840000 | tf_op jit(solution)/shard_map/all_to_all | solution.py:34
  16.5 0.6 copy.14
  17.1 82.3 %all_to_all.38 = bf16[48,32,625]{2,0,1:T(8,128)(2,1)} all-to-all(bf16[48,32,625]{2,0,1:T(8,128)(2,1)S(1)} %copy.14), channel_id=1, replica_groups=mesh['row'=32,'col'=8] {'row'}, dimensions={1} | all-to-all | bytes 3840000 | tf_op jit(solution)/shard_map/all_to_all | solution.py:34
  99.4 0.0 all-gather.5.cloned.1.call-update
  99.4 5.3 %all-gather.3.cloned.1.call-done = bf16[1536,2048]{1,0:T(8,128)(2,1)} async-done(((bf16[48,2048]{1,0:T(8,128)(2,1)}), bf16[1536,2048]{1,0:T(8,128)(2,1)}) %all-gather.3.cloned.1.call-update) | async-done | bytes 6291472 | tf_op jit(solution)/shard_map/all_gather | solution.py:36
  104.7 8.7 %copy.12 = bf16[1536,2048]{0,1:T(8,128)(2,1)} copy(bf16[1536,2048]{1,0:T(8,128)(2,1)} %all-gather.3.cloned.1.call-done) | data formatting | bytes 12582912 | tf_op jit(solution)/shard_map/all_gather | solution.py:36
  113.3 145.5 %all_to_all.39 = bf16[1536,8,256]{0,2,1:T(8,128)(2,1)} all-to-all(bf16[1536,8,256]{0,2,1:T(8,128)(2,1)} %bitcast.12), channel_id=1, replica_groups=mesh['row'=32,'col'=8] {'col'}, dimensions={1} | all-to-all | bytes 12582912 | tf_op jit(solution)/shard_map/all_to_all | solution.py:37
  258.8 8.7 %copy.13 = bf16[8,1536,256]{2,1,0:T(8,128)(2,1)} copy(bf16[8,1536,256]{1,2,0:T(8,128)(2,1)} %bitcast.13) | data formatting | bytes 12582912 | tf_op jit(solution)/shard_map/all_to_all | solution.py:37
  267.5 72.1 %all-gather.5.cloned.1.call-done = bf16[12288,625]{1,0:T(8,128)(2,1)} async-done(((bf16[1536,625]{1,0:T(8,128)(2,1)}), bf16[12288,625]{1,0:T(8,128)(2,1)}) %all-gather.5.cloned.1.call-update) | async-done | bytes 15360016 | tf_op jit(solution)/shard_map/all_gather | solution.py:40
  339.6 14.3 %fusion = f32[256,625]{0,1:T(8,128)} fusion(bf16[12288,256]{1,0:T(8,128)(2,1)} %bitcast.15, bf16[12288,625]{1,0:T(8,128)(2,1)} %all-gather.5.cloned.1.call-done), kind=kOutput, calls=%fused_computation.8 | convolution fusion | flops 3932160000 | bytes 22291456 | tf_op jit(solution)/shard_map/dot_general | solution.py:38
  (1 shorter events, 0.0 us)
Async XLA Ops:
  6.5 98.1 %all-gather.3.cloned.1.call-start = ((), (), s32[]{:S(2)}) async-start(), calls=%async_computation.2 | async-start | bytes 6488064 | tf_op jit(solution)/shard_map/all_gather | solution.py:36
  10.7 328.9 %all-gather.5.cloned.1.call-start = ((), (), s32[]{:S(2)}) async-start(), calls=%async_computation.3 | async-start | bytes 17694720 | tf_op jit(solution)/shard_map/all_gather | solution.py:40
Sparse Core Ops, SparseCore 0:
  10.9 93.7 all-gather.2
  106.5 233.0 all-gather.4
where the time goes:
time: 361 us
  blocking collectives  228 us (63%)
  waiting for transfers between devices  77.4 us (21%)
  local copies, waits for them, and re-layouts  24.4 us (7%)
  matrix products  14.3 us (4%)
  between operations  13.4 us (4%)
    all_to_all x1, blocking collectives, shards(): lax.all_to_all(slab_group, 'col', split_axis=1, concat_axis=0, tiled=True)  145 us
    all_to_all x1, blocking collectives, shards(): lax.all_to_all(pair_elems, 'row', split_axis=1, concat_axis=0, tiled=True)  82.3 us
    all_gather x1, waiting for transfers between devices, shards(): lax.all_gather(row_block, 'col', axis=0, tiled=True)  72.1 us
    dot_general x1, matrix products, shards(): lax.dot_general(panels, lax.all_gather(row_block, 'col', axis=0, tiled=Tr...  14.3 us
    all_gather x1, local copies, waits for them, and re-layouts, shards(): slab_group = lax.all_gather(weighted, 'row', axis=0, tiled=True)  8.68 us
    all_to_all x1, local copies, waits for them, and re-layouts, shards(): lax.all_to_all(slab_group, 'col', split_axis=1, concat_axis=0, tiled=True)  8.67 us
  transfers between devices with their start and end apart: 2, of which 2 were waited for; matrix products, arithmetic and copies ran while one was open for 5% of the time, Pallas kernels for 0%

commit v1 on v0

v1 whole, which is shorter than its diff:
```python
import jax
import jax.numpy as jnp
from jax import lax
from jax.experimental import pallas as pl
from jax.experimental.pallas import tpu as pltpu
from jax.sharding import PartitionSpec as P

MESH = pl.DeviceIdType.MESH
NCOL = 2048
NG = 20000
GBLK = 625
QUART = 160
PAIRS = 48
NCH = 5
CH = 128
HALF = 1024


def body(pe, bands, val, con, out, tail, a_all, b_st, b_rc, c_acc, s_st, s_rc, f_st, gath,
         a_ss, a_rs, b_ss, b_rs, z_ss, z_rs, x_ss, x_rs, l_sem):
    row, col = lax.axis_index("row"), lax.axis_index("col")
    x, y, c = col % 4, row // 8, row % 2
    z = ((row // 2) % 4) * 2 + col // 4

    def dev(px, py, pz, pc):
        return (py * 8 + (pz // 2) * 2 + pc, (pz % 2) * 4 + px)

    def slot(px, py, pc):
        return pc * 16 + px * 4 + py

    def near(dx, dy):
        return dev((x + dx) % 4, (y + dy) % 4, z, c)

    offsets = [(dx, dy, dc) for dx, dy in ORDER for dc in range(2)] + [(0, 0, 1)]
    plane = [(lax.rem(x + dx, 4), lax.rem(y + dy, 4), lax.rem(c + dc, 2)) for dx, dy, dc in offsets]
    up, down = dev(x, y, (z + 1) % 8, c), dev(x, y, (z + 7) % 8, c)

    barrier = pltpu.get_barrier_semaphore()
    for px, py, pc in plane:
        pl.semaphore_signal(barrier, inc=1, device_id=dev(px, py, z, pc), device_id_type=MESH)
    for t in (up, down):
        pl.semaphore_signal(barrier, inc=1, device_id=t, device_id_type=MESH)

    eye = lax.broadcasted_iota(jnp.int32, (PAIRS, PAIRS), 0) == lax.broadcasted_iota(jnp.int32, (PAIRS, PAIRS), 1)
    bf = bands[...].astype(jnp.float32)

    def as_column(r):
        return jnp.sum(jnp.where(eye, jnp.broadcast_to(r, (PAIRS, PAIRS)), 0.0), axis=1, keepdims=True)

    def look_up(ids, table):
        n = table.shape[1]
        lanes = lax.broadcasted_iota(jnp.int32, (PAIRS, n), 1).astype(jnp.float32)
        return jnp.sum(jnp.where(ids == lanes, jnp.broadcast_to(table, (PAIRS, n)), 0.0), axis=1, keepdims=True)

    valence = look_up(as_column(bf[0:1]), val[...])
    conduct = look_up(as_column(bf[1:2]), con[...])
    weights = -4.0 / (conduct - valence)
    me = slot(x, y, c)
    mine = pl.multiple_of(me * PAIRS, 16)
    a_all[pl.ds(mine, PAIRS), :] = (weights * pe[:, :NCOL].astype(jnp.float32)).astype(jnp.bfloat16)

    pl.semaphore_wait(barrier, len(plane) + 2)

    index = {}

    def piece(px, py, cols):
        r = pl.multiple_of(slot(px, py, c) * PAIRS, 16)
        return a_all.at[pl.ds(r, PAIRS), pl.ds(cols[0], cols[1])]

    def a_copy(key, px, py, cols, target):
        i = index.setdefault(key, len(index))
        ref = piece(px, py, cols)
        return pltpu.make_async_remote_copy(src_ref=ref, dst_ref=ref, send_sem=a_ss.at[i], recv_sem=a_rs.at[i],
                                            device_id=target, device_id_type=MESH)

    sent = []

    def a_send(key, px, py, cols, target):
        cp = a_copy(key, px, py, cols, target)
        cp.start()
        sent.append(cp)

    def a_wait(key, px, py, cols):
        a_copy(key, px, py, cols, near(1, 0)).wait_recv()

    def at(h, d1, d2):
        dx, dy = (d1, d2) if h == 0 else (d2, d1)
        return (x + dx) % 4, (y + dy) % 4

    def to(h, d1, d2):
        px, py = at(h, d1, d2)
        return dev(px, py, z, c)

    full = {0: (0, 1024), 1: (1024, 1024)}
    part = {(h, s): (h * 1024 + (0 if s == 1 else 512), 512) for h in (0, 1) for s in (1, 3)}
    for h in (0, 1):
        for s in (1, 3):
            a_send(("p1", h, s), x, y, full[h], to(h, s, 0))
    for h in (0, 1):
        for s in (1, 3):
            a_send(("p2", h, 0, s), x, y, full[h], to(h, 0, s))

    tail[...] = jnp.zeros_like(tail)
    tail[:, 0:32] = pe[:, NG - 32:NG]
    lane = lax.broadcasted_iota(jnp.int32, (PAIRS, CH), 1)

    def source(tile):
        v = tail[...] if tile == NG // CH else pe[:, tile * CH:(tile + 1) * CH]
        return v.astype(jnp.float32)

    def stage(t):
        for pc in range(2):
            for px in range(4):
                for py in range(4):
                    acc = None
                    for zh in range(4):
                        start = (py * 8 + zh * 2 + pc) * GBLK + px * QUART + t * 32
                        tile, off = start // CH, start % CH
                        shift = (32 * zh - off) % CH
                        v = pltpu.roll(source(tile), shift, 1)
                        if off > 96 and tile < NG // CH:
                            v = jnp.where(lane < 32 * zh + CH - off, v, pltpu.roll(source(tile + 1), shift, 1))
                        acc = v if acc is None else jnp.where(lane < 32 * zh, acc, v)
                    b_st[t, slot(px, py, pc)] = acc.astype(jnp.bfloat16)

    def b_send(t):
        for px, py, pc in plane:
            pltpu.make_async_remote_copy(
                src_ref=b_st.at[t, slot(px, py, pc)], dst_ref=b_rc.at[t, pl.ds(mine, PAIRS)],
                send_sem=b_ss.at[t], recv_sem=b_rs.at[t], device_id=dev(px, py, z, pc), device_id_type=MESH).start()

    def b_done(t):
        return pltpu.make_async_remote_copy(
            src_ref=b_rc.at[t, pl.ds(0, 31 * PAIRS)], dst_ref=b_rc.at[t, pl.ds(0, 31 * PAIRS)],
            send_sem=b_ss.at[t], recv_sem=b_rs.at[t], device_id=near(1, 0), device_id_type=MESH)

    for t in range(NCH):
        stage(t)
        b_rc[t, pl.ds(mine, PAIRS)] = b_st[t, me]

    for s in (1, 3):
        for h in (0, 1):
            px, py = at(h, -s, 0)
            a_wait(("p1", h, s), px, py, full[h])
            a_send(("f1", h, s), px, py, part[h, s], to(h, s, 0))
            for u in (1, 3):
                a_send(("p2", h, s, u), px, py, full[h], to(h, 0, u))
    for s in (1, 3):
        for h in (0, 1):
            px, py = at(h, 2, 0)
            a_wait(("f1", h, s), px, py, part[h, s])
            for u in (1, 3):
                a_send(("p2q", h, s, u), px, py, part[h, s], to(h, 0, u))
    for q in (0, 1, 3):
        for u in (1, 3):
            for h in (0, 1):
                px, py = at(h, -q, -u)
                a_wait(("p2", h, q, u), px, py, full[h])
                a_send(("f2", h, q, u), px, py, part[h, u], to(h, 0, u))
    for u in (1, 3):
        for s in (1, 3):
            for h in (0, 1):
                px, py = at(h, 2, -u)
                a_wait(("p2q", h, s, u), px, py, part[h, s])
                if s == u:
                    a_send(("f2", h, 2, u), px, py, part[h, u], to(h, 0, u))
    for t in range(NCH):
        b_send(t)
    for q in (0, 1, 3, 2):
        for u in (1, 3):
            for h in (0, 1):
                px, py = at(h, -q, 2)
                a_wait(("f2", h, q, u), px, py, part[h, u])
    own = pl.multiple_of(c * 16 * PAIRS, 16)
    i = len(index)
    theirs = a_all.at[pl.ds(own, 16 * PAIRS)]
    sib = pltpu.make_async_remote_copy(src_ref=theirs, dst_ref=theirs, send_sem=a_ss.at[i], recv_sem=a_rs.at[i],
                                       device_id=dev(x, y, z, 1 - c), device_id_type=MESH)
    sib.start()
    sent.append(sib)
    sib.wait_recv()

    def multiply(t):
        bt = b_rc[t].T

        def columns(n, carry):
            w = pl.ds(pl.multiple_of(n * 512, 512), 512)
            c_acc[t, :, w] = jnp.dot(bt, a_all[:, w], preferred_element_type=jnp.float32)
            return carry

        lax.fori_loop(0, NCOL // 512, columns, 0)

    def z_copy(t, d, s):
        rows = pl.ds(16 * d, 16) if s == 0 else pl.ds(0, 32)
        return pltpu.make_async_remote_copy(
            src_ref=s_st.at[t, d, s, rows], dst_ref=s_rc.at[t, d, s, rows], send_sem=z_ss.at[t, d, s],
            recv_sem=z_rs.at[t, d, s], device_id=(down, up)[d], device_id_type=MESH)

    def own_part(t, dz):
        goal = (z + dz) % 8
        return c_acc[t, pl.ds(pl.multiple_of((goal // 2) * 32, 32), 32),
                     pl.ds(pl.multiple_of((goal % 2) * HALF, HALF), HALF)]

    def x_copy(t, dx):
        px = (x + dx) % 4
        return pltpu.make_async_remote_copy(
            src_ref=f_st.at[t, :, pl.ds(pl.multiple_of(px * 256, 256), 256)],
            dst_ref=gath.at[pl.ds(pl.multiple_of(x * QUART + t * 32, 32), 32)],
            send_sem=x_ss.at[t], recv_sem=x_rs.at[t], device_id=dev(px, y, z, c), device_id_type=MESH)

    def x_done(t):
        return pltpu.make_async_remote_copy(
            src_ref=gath.at[pl.ds(0, 96)], dst_ref=gath.at[pl.ds(0, 96)],
            send_sem=x_ss.at[t], recv_sem=x_rs.at[t], device_id=near(1, 0), device_id_type=MESH)

    def reduce_step(t, s):
        if s == 0:
            v = own_part(t, 4).astype(jnp.bfloat16)
            for d in (0, 1):
                s_st[t, d, 0, 16 * d:16 * d + 16] = v[16 * d:16 * d + 16]
                z_copy(t, d, 0).start()
        elif s < 4:
            for d in (0, 1):
                z_copy(t, d, s - 1).wait_recv()
                v = own_part(t, (s - 4) if d == 0 else (4 - s))
                if s == 1:
                    got = s_rc[t, d, 0, 16 * d:16 * d + 16].astype(jnp.float32)
                    s_st[t, d, 1, 16 * d:16 * d + 16] = (v[16 * d:16 * d + 16] + got).astype(jnp.bfloat16)
                    e = 1 - d
                    s_st[t, d, 1, 16 * e:16 * e + 16] = v[16 * e:16 * e + 16].astype(jnp.bfloat16)
                else:
                    s_st[t, d, s] = (v + s_rc[t, d, s - 1].astype(jnp.float32)).astype(jnp.bfloat16)
                z_copy(t, d, s).start()
        else:
            for d in (0, 1):
                z_copy(t, d, 3).wait_recv()
            f_st[t] = own_part(t, 0) + s_rc[t, 0, 3].astype(jnp.float32) + s_rc[t, 1, 3].astype(jnp.float32)
            for dx in (2, 1, 3):
                x_copy(t, dx).start()
            gath[pl.ds(pl.multiple_of(x * QUART + t * 32, 32), 32)] = f_st[t, :, pl.ds(pl.multiple_of(x * 256, 256), 256)]

    for k in range(NCH + 4):
        for s in (4, 3, 2, 1):
            if 0 <= k - s < NCH:
                reduce_step(k - s, s)
        if k < NCH:
            b_done(k).wait_recv()
            multiply(k)
            reduce_step(k, 0)

    for t in range(NCH):
        x_done(t).wait_recv()
    out[...] = gath[...].T[:, :GBLK]

    for cp in sent:
        cp.wait_send()
    for t in range(NCH):
        b_done(t).wait_send()
        x_done(t).wait_send()
        for d in (0, 1):
            for s in range(4):
                z_copy(t, d, s).wait_send()


ORDER = [(2, 2), (1, 2), (2, 1), (3, 2), (2, 3), (2, 0), (0, 2), (1, 1), (3, 3), (1, 3), (3, 1), (1, 0), (3, 0), (0, 1), (0, 3)]
N_A = 45


def shards(pair_elems, pair_bands, valence_energy, conduction_energy):
    vm = pl.BlockSpec(memory_space=pltpu.VMEM)
    bf, f32, dma = jnp.bfloat16, jnp.float32, pltpu.SemaphoreType.DMA
    return pl.pallas_call(
        body,
        out_shape=jax.ShapeDtypeStruct((256, GBLK), f32),
        in_specs=[vm] * 4,
        out_specs=vm,
        scratch_shapes=[
            pltpu.VMEM((PAIRS, CH), bf),
            pltpu.VMEM((32 * PAIRS, NCOL), bf),
            pltpu.VMEM((NCH, 32, PAIRS, CH), bf),
            pltpu.VMEM((NCH, 32 * PAIRS, CH), bf),
            pltpu.VMEM((NCH, CH, NCOL), f32),
            pltpu.VMEM((NCH, 2, 4, 32, HALF), bf),
            pltpu.VMEM((NCH, 2, 4, 32, HALF), bf),
            pltpu.VMEM((NCH, 32, HALF), f32),
            pltpu.VMEM((4 * QUART, 256), f32),
            dma((N_A,)), dma((N_A,)), dma((NCH,)), dma((NCH,)),
            dma((NCH, 2, 4)), dma((NCH, 2, 4)), dma((NCH,)), dma((NCH,)), dma((1,)),
        ],
        compiler_params=pltpu.CompilerParams(collective_id=0, has_side_effects=True, vmem_limit_bytes=48 * 2**20),
        cost_estimate=pl.CostEstimate(flops=2 * 1536 * 2048 * 640, bytes_accessed=3 * 2**20, transcendentals=0),
        name="polar",
    )(pair_elems, pair_bands, valence_energy.reshape(1, -1), conduction_energy.reshape(1, -1))


def solution(mesh):
    placed = (P(("row", "col"), None), P(None, ("row", "col")), P(), P())
    return jax.shard_map(shards, mesh=mesh, in_specs=placed, out_specs=P("col", "row"), check_vma=False)
```

time: 361 us -> 88.9 us (0.25)
  blocking collectives: 228 us -> 0 us
  Pallas kernels: 0 us -> 84.1 us
  waiting for transfers between devices: 77.4 us -> 0 us
  local copies, waits for them, and re-layouts: 24.4 us -> 4.61 us
  matrix products: 14.3 us -> 0 us
  between operations: 13.4 us -> 0.01 us
    all_to_all x2 -> x0, blocking collectives: 228 us -> none  [the longest x1 145 us: shards(): lax.all_to_all(slab_group, 'col', split_axis=1, concat_axis=0, tiled=True)]
    pallas_call x0 -> x1, Pallas kernels: none -> 84.1 us  [shards(): pl.pallas_call(body, out_shape=jax.ShapeDtypeStruct((256, GBLK), f32), in...]
    all_gather x2 -> x0, waiting for transfers between devices: 77.4 us -> none  [the longest x1 72.1 us: shards(): lax.all_gather(row_block, 'col', axis=0, tiled=True)]
    all_to_all x3 -> x0, local copies, waits for them, and re-layouts: 15 us -> none  [the longest x1 8.67 us: shards(): lax.all_to_all(slab_group, 'col', split_axis=1, concat_axis=0, tiled=True)]
    dot_general x1 -> x0, matrix products: 14.3 us -> none  [shards(): lax.dot_general(panels, lax.all_gather(row_block, 'col', axis=0, tiled=Tr...]
    all_gather x1 -> x0, local copies, waits for them, and re-layouts: 8.68 us -> none  [shards(): slab_group = lax.all_gather(weighted, 'row', axis=0, tiled=True)]
  transfers between devices with their start and end apart: 2 -> 0, of which waited for: 2 -> 0; matrix products, arithmetic and copies ran while one was open for 5% -> 0% of each run, Pallas kernels for 0% -> 0%
where the time goes in v1:
time: 88.9 us; the launch traced here: 88.7 us
  Pallas kernels  84.1 us (95%)
  local copies, waits for them, and re-layouts  4.61 us (5%)
    pallas_call x1, Pallas kernels, shards(): pl.pallas_call(body, out_shape=jax.ShapeDtypeStruct((256, GBLK), f32), in...  84.1 us
    unnamed x8, local copies, waits for them, and re-layouts  3.54 us

profile of v1, /device:TPU:1, one launch (start us, length us, event | category | flops | bytes accessed | tf_op | source)
XLA Modules:
  0.0 88.7 jit_solution(10642004144839926755)
XLA Ops:
  0.0 0.0 copy-start
  0.0 1.5 %copy-done = bf16[48,20000]{1,0:T(8,128)(2,1)S(1)} copy-done((bf16[48,20000]{1,0:T(8,128)(2,1)S(1)}, bf16[48,20000]{1,0:T(8,128)(2,1)}, u32[]{:S(2)}) %copy-start) | copy-done | bytes 1920024
  1.5 0.0 copy-start.1
  1.5 0.7 copy-done.1
  2.2 0.0 copy-start.2
  2.2 0.7 copy-done.2
  2.9 0.0 copy-start.3
  2.9 0.7 copy-done.3
  3.5 84.1 %polar.1 = f32[256,625]{1,0:T(8,128)S(1)} custom-call(bf16[48,20000]{1,0:T(8,128)(2,1)S(1)} %copy-done, s32[2,48]{1,0:T(2,128)S(1)} %copy-done.1, f32[1,48]{1,0:T(1,128)S(1)} %bitcast.3, f32[1,256]{1,0:T(1,128)S(1)} %bitcast.2), custom_call_target="tpu_custom_call" | custom-call | flops 4026531840 | bytes 3145728 | tf_op jit(solution)/shard_map/polar/pallas_call | solution.py:272
  87.7 1.1 %copy.5 = f32[256,625]{0,1:T(8,128)} copy(f32[256,625]{1,0:T(8,128)S(1)} %polar.1) | data formatting | bytes 1280000 | tf_op jit(solution)/shard_map/polar/pallas_call | solution.py:272
Async XLA Ops:
  0.0 1.5 %copy-start = (bf16[48,20000]{1,0:T(8,128)(2,1)S(1)}, bf16[48,20000]{1,0:T(8,128)(2,1)}, u32[]{:S(2)}) copy-start(bf16[48,20000]{1,0:T(8,128)(2,1)} %pe.1) | copy-start | bytes 5760004
  1.5 0.7 copy-start.1
  2.2 0.7 copy-start.2
  2.9 0.7 copy-start.3

commit v2 on v1

--- a/solution.py
+++ b/solution.py
@@ -16,8 +16,8 @@
 HALF = 1024
 
 
-def body(pe, bands, val, con, out, tail, a_all, b_st, b_rc, c_acc, s_st, s_rc, f_st, gath,
-         a_ss, a_rs, b_ss, b_rs, z_ss, z_rs, x_ss, x_rs, l_sem):
+def body(pe_hbm, bands_hbm, val_hbm, con_hbm, out, pe, slab, bands, val, con, tail, a_all, b_st, b_rc, b_t, c_acc, s_st, s_rc, f_st, gath,
+         a_ss, a_rs, b_ss, b_rs, z_ss, z_rs, x_ss, x_rs, c_ss, c_rs, l_sem):
     row, col = lax.axis_index("row"), lax.axis_index("col")
     x, y, c = col % 4, row // 8, row % 2
     z = ((row // 2) % 4) * 2 + col // 4
@@ -41,6 +41,13 @@
     for t in (up, down):
         pl.semaphore_signal(barrier, inc=1, device_id=t, device_id_type=MESH)
 
+    loads = [pltpu.make_async_copy(src, dst, l_sem.at[i]) for i, (src, dst) in enumerate([
+        (bands_hbm, bands), (val_hbm, val), (con_hbm, con), (pe_hbm.at[:, pl.ds(0, NCOL)], slab), (pe_hbm, pe)])]
+    for cp in loads:
+        cp.start()
+    for cp in loads[:3]:
+        cp.wait()
+
     eye = lax.broadcasted_iota(jnp.int32, (PAIRS, PAIRS), 0) == lax.broadcasted_iota(jnp.int32, (PAIRS, PAIRS), 1)
     bf = bands[...].astype(jnp.float32)
 
@@ -57,7 +64,8 @@
     weights = -4.0 / (conduct - valence)
     me = slot(x, y, c)
     mine = pl.multiple_of(me * PAIRS, 16)
-    a_all[pl.ds(mine, PAIRS), :] = (weights * pe[:, :NCOL].astype(jnp.float32)).astype(jnp.bfloat16)
+    loads[3].wait()
+    a_all[pl.ds(mine, PAIRS), :] = (weights * slab[...].astype(jnp.float32)).astype(jnp.bfloat16)
 
     pl.semaphore_wait(barrier, len(plane) + 2)
 
@@ -90,6 +98,11 @@
     def to(h, d1, d2):
         px, py = at(h, d1, d2)
         return dev(px, py, z, c)
+
+    def core_copy(px, py, h):
+        ref = piece(px, py, full[h])
+        return pltpu.make_async_remote_copy(src_ref=ref, dst_ref=ref, send_sem=c_ss.at[0], recv_sem=c_rs.at[0],
+                                            device_id=dev(x, y, z, 1 - c), device_id_type=MESH)
 
     full = {0: (0, 1024), 1: (1024, 1024)}
     part = {(h, s): (h * 1024 + (0 if s == 1 else 512), 512) for h in (0, 1) for s in (1, 3)}
@@ -99,7 +112,10 @@
     for h in (0, 1):
         for s in (1, 3):
             a_send(("p2", h, 0, s), x, y, full[h], to(h, 0, s))
-
+    for h in (0, 1):
+        core_copy(x, y, h).start()
+
+    loads[4].wait()
     tail[...] = jnp.zeros_like(tail)
     tail[:, 0:32] = pe[:, NG - 32:NG]
     lane = lax.broadcasted_iota(jnp.int32, (PAIRS, CH), 1)
@@ -145,18 +161,22 @@
             a_send(("f1", h, s), px, py, part[h, s], to(h, s, 0))
             for u in (1, 3):
                 a_send(("p2", h, s, u), px, py, full[h], to(h, 0, u))
+            core_copy(px, py, h).start()
     for s in (1, 3):
         for h in (0, 1):
             px, py = at(h, 2, 0)
             a_wait(("f1", h, s), px, py, part[h, s])
             for u in (1, 3):
                 a_send(("p2q", h, s, u), px, py, part[h, s], to(h, 0, u))
+            if s == 3:
+                core_copy(px, py, h).start()
     for q in (0, 1, 3):
         for u in (1, 3):
             for h in (0, 1):
                 px, py = at(h, -q, -u)
                 a_wait(("p2", h, q, u), px, py, full[h])
                 a_send(("f2", h, q, u), px, py, part[h, u], to(h, 0, u))
+                core_copy(px, py, h).start()
     for u in (1, 3):
         for s in (1, 3):
             for h in (0, 1):
@@ -164,48 +184,49 @@
                 a_wait(("p2q", h, s, u), px, py, part[h, s])
                 if s == u:
                     a_send(("f2", h, 2, u), px, py, part[h, u], to(h, 0, u))
-    for t in range(NCH):
+                if s == 3:
+                    core_copy(px, py, h).start()
+    for t in range(WIN):
         b_send(t)
     for q in (0, 1, 3, 2):
         for u in (1, 3):
             for h in (0, 1):
                 px, py = at(h, -q, 2)
                 a_wait(("f2", h, q, u), px, py, part[h, u])
+                if u == 3:
+                    core_copy(px, py, h).start()
     own = pl.multiple_of(c * 16 * PAIRS, 16)
-    i = len(index)
-    theirs = a_all.at[pl.ds(own, 16 * PAIRS)]
-    sib = pltpu.make_async_remote_copy(src_ref=theirs, dst_ref=theirs, send_sem=a_ss.at[i], recv_sem=a_rs.at[i],
-                                       device_id=dev(x, y, z, 1 - c), device_id_type=MESH)
-    sib.start()
-    sent.append(sib)
-    sib.wait_recv()
-
-    def multiply(t):
-        bt = b_rc[t].T
-
-        def columns(n, carry):
-            w = pl.ds(pl.multiple_of(n * 512, 512), 512)
-            c_acc[t, :, w] = jnp.dot(bt, a_all[:, w], preferred_element_type=jnp.float32)
-            return carry
-
-        lax.fori_loop(0, NCOL // 512, columns, 0)
-
-    def z_copy(t, d, s):
-        rows = pl.ds(16 * d, 16) if s == 0 else pl.ds(0, 32)
+    theirs = a_all.at[pl.ds(pl.multiple_of((1 - c) * 16 * PAIRS, 16), 16 * PAIRS)]
+    ours = a_all.at[pl.ds(own, 16 * PAIRS)]
+    core_done = pltpu.make_async_remote_copy(src_ref=ours, dst_ref=theirs, send_sem=c_ss.at[0], recv_sem=c_rs.at[0],
+                                             device_id=dev(x, y, z, 1 - c), device_id_type=MESH)
+    core_done.wait_recv()
+
+    def multiply(t, n):
+        if n == 0:
+            b_t[t] = b_rc[t].T
+        w = slice(n * 512, n * 512 + 512)
+        c_acc[t, :, w] = jnp.dot(b_t[t], a_all[:, w], preferred_element_type=jnp.float32)
+
+    UR = 32 // SPLIT
+
+    def z_copy(t, h, d, s):
+        cols = pl.ds(512 * d, 512) if s == 0 else pl.ds(0, HALF)
+        ref = (t, h, d, s, pl.ds(0, UR), cols)
         return pltpu.make_async_remote_copy(
-            src_ref=s_st.at[t, d, s, rows], dst_ref=s_rc.at[t, d, s, rows], send_sem=z_ss.at[t, d, s],
-            recv_sem=z_rs.at[t, d, s], device_id=(down, up)[d], device_id_type=MESH)
-
-    def own_part(t, dz):
+            src_ref=s_st.at[ref], dst_ref=s_rc.at[ref], send_sem=z_ss.at[t, h, d, s],
+            recv_sem=z_rs.at[t, h, d, s], device_id=(down, up)[d], device_id_type=MESH)
+
+    def own_part(t, h, dz):
         goal = (z + dz) % 8
-        return c_acc[t, pl.ds(pl.multiple_of((goal // 2) * 32, 32), 32),
+        return c_acc[t, pl.ds(pl.multiple_of((goal // 2) * 32 + h * UR, UR), UR),
                      pl.ds(pl.multiple_of((goal % 2) * HALF, HALF), HALF)]
 
-    def x_copy(t, dx):
+    def x_copy(t, h, dx):
         px = (x + dx) % 4
         return pltpu.make_async_remote_copy(
-            src_ref=f_st.at[t, :, pl.ds(pl.multiple_of(px * 256, 256), 256)],
-            dst_ref=gath.at[pl.ds(pl.multiple_of(x * QUART + t * 32, 32), 32)],
+            src_ref=f_st.at[t, pl.ds(h * UR, UR), pl.ds(pl.multiple_of(px * 256, 256), 256)],
+            dst_ref=gath.at[pl.ds(pl.multiple_of(x * QUART + t * 32 + h * UR, UR), UR)],
             send_sem=x_ss.at[t], recv_sem=x_rs.at[t], device_id=dev(px, y, z, c), device_id_type=MESH)
 
     def x_done(t):
@@ -213,40 +234,44 @@
             src_ref=gath.at[pl.ds(0, 96)], dst_ref=gath.at[pl.ds(0, 96)],
             send_sem=x_ss.at[t], recv_sem=x_rs.at[t], device_id=near(1, 0), device_id_type=MESH)
 
-    def reduce_step(t, s):
+    def reduce_step(t, h, s):
         if s == 0:
-            v = own_part(t, 4).astype(jnp.bfloat16)
+            v = own_part(t, h, 4).astype(jnp.bfloat16)
             for d in (0, 1):
-                s_st[t, d, 0, 16 * d:16 * d + 16] = v[16 * d:16 * d + 16]
-                z_copy(t, d, 0).start()
+                s_st[t, h, d, 0, :, 512 * d:512 * d + 512] = v[:, 512 * d:512 * d + 512]
+                z_copy(t, h, d, 0).start()
         elif s < 4:
             for d in (0, 1):
-                z_copy(t, d, s - 1).wait_recv()
-                v = own_part(t, (s - 4) if d == 0 else (4 - s))
+                z_copy(t, h, d, s - 1).wait_recv()
+                v = own_part(t, h, (s - 4) if d == 0 else (4 - s))
                 if s == 1:
-                    got = s_rc[t, d, 0, 16 * d:16 * d + 16].astype(jnp.float32)
-                    s_st[t, d, 1, 16 * d:16 * d + 16] = (v[16 * d:16 * d + 16] + got).astype(jnp.bfloat16)
                     e = 1 - d
-                    s_st[t, d, 1, 16 * e:16 * e + 16] = v[16 * e:16 * e + 16].astype(jnp.bfloat16)
+                    got = s_rc[t, h, d, 0, :, 512 * d:512 * d + 512].astype(jnp.float32)
+                    s_st[t, h, d, 1, :, 512 * d:512 * d + 512] = (v[:, 512 * d:512 * d + 512] + got).astype(jnp.bfloat16)
+                    s_st[t, h, d, 1, :, 512 * e:512 * e + 512] = v[:, 512 * e:512 * e + 512].astype(jnp.bfloat16)
                 else:
-                    s_st[t, d, s] = (v + s_rc[t, d, s - 1].astype(jnp.float32)).astype(jnp.bfloat16)
-                z_copy(t, d, s).start()
+                    s_st[t, h, d, s] = (v + s_rc[t, h, d, s - 1].astype(jnp.float32)).astype(jnp.bfloat16)
+                z_copy(t, h, d, s).start()
         else:
             for d in (0, 1):
-                z_copy(t, d, 3).wait_recv()
-            f_st[t] = own_part(t, 0) + s_rc[t, 0, 3].astype(jnp.float32) + s_rc[t, 1, 3].astype(jnp.float32)
+                z_copy(t, h, d, 3).wait_recv()
+            total = own_part(t, h, 0) + s_rc[t, h, 0, 3].astype(jnp.float32) + s_rc[t, h, 1, 3].astype(jnp.float32)
+            f_st[t, h * UR:h * UR + UR] = total
             for dx in (2, 1, 3):
-                x_copy(t, dx).start()
-            gath[pl.ds(pl.multiple_of(x * QUART + t * 32, 32), 32)] = f_st[t, :, pl.ds(pl.multiple_of(x * 256, 256), 256)]
-
-    for k in range(NCH + 4):
-        for s in (4, 3, 2, 1):
-            if 0 <= k - s < NCH:
-                reduce_step(k - s, s)
-        if k < NCH:
+                x_copy(t, h, dx).start()
+            gath[pl.ds(pl.multiple_of(x * QUART + t * 32 + h * UR, UR), UR)] = (
+                f_st[t, h * UR:h * UR + UR, pl.ds(pl.multiple_of(x * 256, 256), 256)])
+
+    for op in plan():
+        if op[0] == "b":
+            k = op[1]
             b_done(k).wait_recv()
-            multiply(k)
-            reduce_step(k, 0)
+            if k + WIN < NCH:
+                b_send(k + WIN)
+        elif op[0] == "m":
+            multiply(*op[1:])
+        else:
+            reduce_step(*op[1:])
 
     for t in range(NCH):
         x_done(t).wait_recv()
@@ -254,16 +279,54 @@
 
     for cp in sent:
         cp.wait_send()
+    core_done.wait_send()
+    for t in range(NCH):
+        x_done(t).wait_send()
+        for h in range(SPLIT):
+            for d in (0, 1):
+                for s in range(4):
+                    z_copy(t, h, d, s).wait_send()
     for t in range(NCH):
         b_done(t).wait_send()
-        x_done(t).wait_send()
-        for d in (0, 1):
-            for s in range(4):
-                z_copy(t, d, s).wait_send()
 
 
 ORDER = [(2, 2), (1, 2), (2, 1), (3, 2), (2, 3), (2, 0), (0, 2), (1, 1), (3, 3), (1, 3), (3, 1), (1, 0), (3, 0), (0, 1), (0, 3)]
-N_A = 45
+N_A = 44
+WIN = 2
+SPLIT = 2
+B_GAP, WIRE, LATENCY, MULTIPLY, STEP, FINAL = 4.2, 1.43, 2.5, 0.45, 0.15, 0.3
+
+
+def plan():
+    came = {("b", k): k * B_GAP for k in range(NCH)}
+    todo = [("b", k) for k in range(NCH)] + [("m", k, n) for k in range(NCH) for n in range(4)]
+    todo += [("r", k, h, s) for k in range(NCH) for h in range(SPLIT) for s in range(5)]
+    done, free, now, order = {}, 0.0, 0.0, []
+
+    def ready(op):
+        if op[0] == "b":
+            return came[op] if all(("b", j) in done for j in range(op[1])) else None
+        if op[0] == "m":
+            need = [("b", op[1])] + [o for o in todo if o[0] == "m" and o < op]
+            return max(done[o] for o in need) if all(o in done for o in need) else None
+        return done.get(("m", op[1], 3)) if op[3] == 0 else came.get(("r",) + op[1:3] + (op[3] - 1,))
+
+    def rank(op):
+        return (0, op[1]) if op[0] == "b" else (1, -op[3], op[1], op[2]) if op[0] == "r" else (2,) + op[1:]
+
+    while todo:
+        times = [(ready(op), op) for op in todo]
+        times = [(t, op) for t, op in times if t is not None]
+        now = max(now, min(t for t, _ in times))
+        op = min((o for t, o in times if t <= now), key=rank)
+        now += 0.3 if op[0] == "b" else MULTIPLY if op[0] == "m" else FINAL if op[3] == 4 else STEP
+        done[op] = now
+        todo.remove(op)
+        order.append(op)
+        if op[0] == "r" and op[3] < 4:
+            free = max(free, now) + WIRE / SPLIT * (0.5 if op[3] == 0 else 1)
+            came[op] = free + LATENCY
+    return order
 
 
 def shards(pair_elems, pair_bands, valence_energy, conduction_energy):
@@ -272,20 +335,26 @@
     return pl.pallas_call(
         body,
         out_shape=jax.ShapeDtypeStruct((256, GBLK), f32),
-        in_specs=[vm] * 4,
+        in_specs=[pl.BlockSpec(memory_space=pltpu.HBM)] * 4,
         out_specs=vm,
         scratch_shapes=[
+            pltpu.VMEM((PAIRS, NG), bf),
+            pltpu.VMEM((PAIRS, NCOL), bf),
+            pltpu.VMEM((2, PAIRS), jnp.int32),
+            pltpu.VMEM((1, 48), f32),
+            pltpu.VMEM((1, 256), f32),
             pltpu.VMEM((PAIRS, CH), bf),
             pltpu.VMEM((32 * PAIRS, NCOL), bf),
             pltpu.VMEM((NCH, 32, PAIRS, CH), bf),
             pltpu.VMEM((NCH, 32 * PAIRS, CH), bf),
+            pltpu.VMEM((NCH, CH, 32 * PAIRS), bf),
             pltpu.VMEM((NCH, CH, NCOL), f32),
-            pltpu.VMEM((NCH, 2, 4, 32, HALF), bf),
-            pltpu.VMEM((NCH, 2, 4, 32, HALF), bf),
+            pltpu.VMEM((NCH, SPLIT, 2, 4, 32 // SPLIT, HALF), bf),
+            pltpu.VMEM((NCH, SPLIT, 2, 4, 32 // SPLIT, HALF), bf),
             pltpu.VMEM((NCH, 32, HALF), f32),
             pltpu.VMEM((4 * QUART, 256), f32),
             dma((N_A,)), dma((N_A,)), dma((NCH,)), dma((NCH,)),
-            dma((NCH, 2, 4)), dma((NCH, 2, 4)), dma((NCH,)), dma((NCH,)), dma((1,)),
+            dma((NCH, SPLIT, 2, 4)), dma((NCH, SPLIT, 2, 4)), dma((NCH,)), dma((NCH,)), dma((1,)), dma((1,)), dma((5,)),
         ],
         compiler_params=pltpu.CompilerParams(collective_id=0, has_side_effects=True, vmem_limit_bytes=48 * 2**20),
         cost_estimate=pl.CostEstimate(flops=2 * 1536 * 2048 * 640, bytes_accessed=3 * 2**20, transcendentals=0),

time: 88.9 us -> 80.8 us (0.909); the launches traced: 88.7 us -> 79.5 us
  Pallas kernels: 84.1 us -> 74.8 us
    pallas_call x1, Pallas kernels: 84.1 us -> 74.8 us  [shards(): pl.pallas_call(body, out_shape=jax.ShapeDtypeStruct((256, GBLK), f32), in...]
where the time goes in v2:
time: 80.8 us; the launch traced here: 79.5 us
  Pallas kernels  74.8 us (93%)
  local copies, waits for them, and re-layouts  4.61 us (6%)
    pallas_call x1, Pallas kernels, shards(): pl.pallas_call(body, out_shape=jax.ShapeDtypeStruct((256, GBLK), f32), in...  74.8 us
    unnamed x8, local copies, waits for them, and re-layouts  3.54 us

profile of v2, /device:TPU:1, one launch (start us, length us, event | category | flops | bytes accessed | tf_op | source)
XLA Modules:
  0.0 79.5 jit_solution(18359691944897726404)
XLA Ops:
  0.0 0.0 copy-start
  0.0 1.5 %copy-done = bf16[48,20000]{1,0:T(8,128)(2,1)S(1)} copy-done((bf16[48,20000]{1,0:T(8,128)(2,1)S(1)}, bf16[48,20000]{1,0:T(8,128)(2,1)}, u32[]{:S(2)}) %copy-start) | copy-done | bytes 1920024
  1.5 0.0 copy-start.1
  1.5 0.7 copy-done.1
  2.2 0.0 copy-start.2
  2.2 0.7 copy-done.2
  2.9 0.0 copy-start.3
  2.9 0.7 copy-done.3
  3.5 74.8 %polar.1 = f32[256,625]{1,0:T(8,128)S(1)} custom-call(bf16[48,20000]{1,0:T(8,128)(2,1)S(1)} %copy-done, s32[2,48]{1,0:T(2,128)S(1)} %copy-done.1, f32[1,48]{1,0:T(1,128)S(1)} %bitcast.3, f32[1,256]{1,0:T(1,128)S(1)} %bitcast.2), custom_call_target="tpu_custom_call" | custom-call | flops 4026531840 | bytes 3145728 | tf_op jit(solution)/shard_map/polar/pallas_call | solution.py:335
  78.4 1.1 %copy.5 = f32[256,625]{0,1:T(8,128)} copy(f32[256,625]{1,0:T(8,128)S(1)} %polar.1) | data formatting | bytes 1280000 | tf_op jit(solution)/shard_map/polar/pallas_call | solution.py:335
Async XLA Ops:
  0.0 1.5 %copy-start = (bf16[48,20000]{1,0:T(8,128)(2,1)S(1)}, bf16[48,20000]{1,0:T(8,128)(2,1)}, u32[]{:S(2)}) copy-start(bf16[48,20000]{1,0:T(8,128)(2,1)} %pe_hbm.1) | copy-start | bytes 5760004
  1.5 0.7 copy-start.1
  2.2 0.7 copy-start.2
  2.9 0.7 copy-start.3

commit v3 on v2

--- a/solution.py
+++ b/solution.py
@@ -35,16 +35,16 @@
     plane = [(lax.rem(x + dx, 4), lax.rem(y + dy, 4), lax.rem(c + dc, 2)) for dx, dy, dc in offsets]
     up, down = dev(x, y, (z + 1) % 8, c), dev(x, y, (z + 7) % 8, c)
 
+    loads = [pltpu.make_async_copy(src, dst, l_sem.at[i]) for i, (src, dst) in enumerate([
+        (bands_hbm, bands), (val_hbm, val), (con_hbm, con), (pe_hbm.at[:, pl.ds(0, NCOL)], slab), (pe_hbm, pe)])]
+    for cp in loads:
+        cp.start()
     barrier = pltpu.get_barrier_semaphore()
     for px, py, pc in plane:
         pl.semaphore_signal(barrier, inc=1, device_id=dev(px, py, z, pc), device_id_type=MESH)
     for t in (up, down):
         pl.semaphore_signal(barrier, inc=1, device_id=t, device_id_type=MESH)
 
-    loads = [pltpu.make_async_copy(src, dst, l_sem.at[i]) for i, (src, dst) in enumerate([
-        (bands_hbm, bands), (val_hbm, val), (con_hbm, con), (pe_hbm.at[:, pl.ds(0, NCOL)], slab), (pe_hbm, pe)])]
-    for cp in loads:
-        cp.start()
     for cp in loads[:3]:
         cp.wait()
 
@@ -201,6 +201,9 @@
     core_done = pltpu.make_async_remote_copy(src_ref=ours, dst_ref=theirs, send_sem=c_ss.at[0], recv_sem=c_rs.at[0],
                                              device_id=dev(x, y, z, 1 - c), device_id_type=MESH)
     core_done.wait_recv()
+    for cp in sent:
+        cp.wait_send()
+    core_done.wait_send()
 
     def multiply(t, n):
         if n == 0:
@@ -262,39 +265,46 @@
             gath[pl.ds(pl.multiple_of(x * QUART + t * 32 + h * UR, UR), UR)] = (
                 f_st[t, h * UR:h * UR + UR, pl.ds(pl.multiple_of(x * 256, 256), 256)])
 
+    ended = []
+
+    def unit_sent(t, h):
+        for d in (0, 1):
+            for s in range(4):
+                z_copy(t, h, d, s).wait_send()
+
     for op in plan():
         if op[0] == "b":
             k = op[1]
             b_done(k).wait_recv()
+            if k > 0:
+                b_done(k - 1).wait_send()
             if k + WIN < NCH:
                 b_send(k + WIN)
         elif op[0] == "m":
             multiply(*op[1:])
         else:
             reduce_step(*op[1:])
+            if op[3] == 4:
+                ended.append(op[1:3])
+                if len(ended) > 2:
+                    unit_sent(*ended[-3])
 
     for t in range(NCH):
         x_done(t).wait_recv()
     out[...] = gath[...].T[:, :GBLK]
 
-    for cp in sent:
-        cp.wait_send()
-    core_done.wait_send()
+    for t, h in ended[-2:]:
+        unit_sent(t, h)
     for t in range(NCH):
         x_done(t).wait_send()
-        for h in range(SPLIT):
-            for d in (0, 1):
-                for s in range(4):
-                    z_copy(t, h, d, s).wait_send()
-    for t in range(NCH):
-        b_done(t).wait_send()
+    b_done(NCH - 1).wait_send()
 
 
 ORDER = [(2, 2), (1, 2), (2, 1), (3, 2), (2, 3), (2, 0), (0, 2), (1, 1), (3, 3), (1, 3), (3, 1), (1, 0), (3, 0), (0, 1), (0, 3)]
 N_A = 44
 WIN = 2
 SPLIT = 2
-B_GAP, WIRE, LATENCY, MULTIPLY, STEP, FINAL = 4.2, 1.43, 2.5, 0.45, 0.15, 0.3
+B_GAP, WIRE, LATENCY, MULTIPLY, STEP, FINAL = 4.2, 1.65, 2.5, 0.45, 0.15, 0.3
 
 
 def plan():

time: 80.8 us -> 80.8 us (level)
  no operation moved by 1% of the time
where the time goes in v3:
time: 80.8 us; the launch traced here: 79.5 us
  Pallas kernels  74.9 us (93%)
  local copies, waits for them, and re-layouts  4.61 us (6%)
    pallas_call x1, Pallas kernels, shards(): pl.pallas_call(body, out_shape=jax.ShapeDtypeStruct((256, GBLK), f32), in...  74.9 us
    unnamed x8, local copies, waits for them, and re-layouts  3.54 us

profile of v3, /device:TPU:1, one launch (start us, length us, event | category | flops | bytes accessed | tf_op | source)
XLA Modules:
  0.0 79.5 jit_solution(7188981536131221223)
XLA Ops:
  0.0 0.0 copy-start
  0.0 1.5 %copy-done = bf16[48,20000]{1,0:T(8,128)(2,1)S(1)} copy-done((bf16[48,20000]{1,0:T(8,128)(2,1)S(1)}, bf16[48,20000]{1,0:T(8,128)(2,1)}, u32[]{:S(2)}) %copy-start) | copy-done | bytes 1920024
  1.5 0.0 copy-start.1
  1.5 0.7 copy-done.1
  2.2 0.0 copy-start.2
  2.2 0.7 copy-done.2
  2.9 0.0 copy-start.3
  2.9 0.7 copy-done.3
  3.5 74.9 %polar.1 = f32[256,625]{1,0:T(8,128)S(1)} custom-call(bf16[48,20000]{1,0:T(8,128)(2,1)S(1)} %copy-done, s32[2,48]{1,0:T(2,128)S(1)} %copy-done.1, f32[1,48]{1,0:T(1,128)S(1)} %bitcast.3, f32[1,256]{1,0:T(1,128)S(1)} %bitcast.2), custom_call_target="tpu_custom_call" | custom-call | flops 4026531840 | bytes 3145728 | tf_op jit(solution)/shard_map/polar/pallas_call | solution.py:345
  78.5 1.1 %copy.5 = f32[256,625]{0,1:T(8,128)} copy(f32[256,625]{1,0:T(8,128)S(1)} %polar.1) | data formatting | bytes 1280000 | tf_op jit(solution)/shard_map/polar/pallas_call | solution.py:345
Async XLA Ops:
  0.0 1.5 %copy-start = (bf16[48,20000]{1,0:T(8,128)(2,1)S(1)}, bf16[48,20000]{1,0:T(8,128)(2,1)}, u32[]{:S(2)}) copy-start(bf16[48,20000]{1,0:T(8,128)(2,1)} %pe_hbm.1) | copy-start | bytes 5760004
  1.5 0.7 copy-start.1
  2.2 0.7 copy-start.2
  2.9 0.7 copy-start.3
